TPU v7x, 32 devices: a whole 2x2x4 slice. The times are simulated.
32 devices in a mesh: grp: 2 (over y), pix: 4 (over z), ori: 2 (over x), pat: 2 (over core).
Axes of the slice: x: 2, y: 2, z: 4, core: 2. Of those that a mesh axis runs over, the one named last changes fastest.
Arguments:
- patterns: bfloat16 [2048, 65536], P(('grp', 'pat'), 'pix'), parts along dimension 0, may hold values from -40 to 40
- model: bfloat16 [131072, 2048], P(('grp', 'pix'), 'ori'), parts along dimension 0, may hold values from -6 to 6
- scale_table: float32 [32], P('grp'), parts along dimension 0, may hold values from 0.5 to 2
- scale_index: int32 [2048], P(('grp', 'pat')), parts along dimension 0, may hold values from 0 to 15
- weight_table: float32 [16], P('grp'), parts along dimension 0, may hold values from -1 to 1
- weight_class: int32 [4096], P(('grp', 'ori')), parts along dimension 0, may hold values from 0 to 7
Outputs:
- new_model: bfloat16 [131072, 2048], P(('grp', 'pix', 'pat'), 'ori'), parts along dimension 0
There are 2 independent parts, one for each index of `grp`. A program takes and returns all parts, laid end to end along the dimension named above; each array names one. Nothing has to cross between parts.
All inputs are finite; a program needn't handle non-finite values.
Results may differ from a plain program's by a relative error of at most 0.0034.
Values may be sent and summed in bfloat16 or wider, within the bound.
A program may use at most 256 MiB of HBM per device.

v0:
```python
import jax
import jax.numpy as jnp
from jax import lax
from jax.sharding import PartitionSpec as P

P_SIZE = 65536


prior_weight = 0.5


def table_lookup(table, index):
    levels = jnp.arange(table.shape[0], dtype=jnp.int32)
    return jnp.sum(jnp.where(index[:, None] == levels[None, :], table[None, :], 0.0), axis=1)


def normalize(scores, phi):
    top = jnp.max(scores, axis=1)
    top = lax.pmax(top, "ori")
    total = lax.psum(jnp.sum(jnp.exp(scores - top[:, None]), axis=1), "ori")
    lse = top + jnp.log(total)
    prob = jnp.exp(scores - lse[:, None])
    weights = (prob * phi[:, None]).astype(jnp.bfloat16)
    den_part = jnp.sum(prob * (phi * phi)[:, None], axis=0)
    return (weights, den_part)


def local(patterns, model, scale_table, scale_index, weight_table, weight_class):
    phi = table_lookup(scale_table, scale_index)
    logw = table_lookup(weight_table, weight_class)
    cross = jnp.dot(patterns, model, preferred_element_type=jnp.float32)
    squares = jnp.sum(jnp.square(model.astype(jnp.float32)), axis=0)
    beta = P_SIZE ** (-0.5)
    partial_term = beta * (phi[:, None] * cross - 0.5 * (phi * phi)[:, None] * squares[None, :])
    share = lax.psum_scatter(partial_term, "pix", scatter_dimension=0, tiled=True)
    count = share.shape[0]
    phi_share = lax.dynamic_slice_in_dim(phi, lax.axis_index("pix") * count, count)
    weights, den_part = normalize(share + logw[None, :], phi_share)
    den = prior_weight + lax.psum(den_part, ("pix", "pat"))
    weights = lax.all_gather(weights, "pix", axis=0, tiled=True)
    half = model.shape[0] // lax.axis_size("pat")
    numer = lax.psum_scatter(
        lax.dot_general(
            patterns, weights, (((0,), (0,)), ((), ())), preferred_element_type=jnp.float32
        ),
        "pat",
        scatter_dimension=0,
        tiled=True,
    )
    own_rows = lax.dynamic_slice_in_dim(model, lax.axis_index("pat") * half, half, 0)
    numer = numer + prior_weight * own_rows.astype(jnp.float32)
    return (numer / den[None, :]).astype(jnp.bfloat16)


def solution(mesh):
    placed = (
        P(("grp", "pat"), "pix"),
        P(("grp", "pix"), "ori"),
        P("grp"),
        P(("grp", "pat")),
        P("grp"),
        P(("grp", "ori")),
    )
    return jax.shard_map(
        local,
        mesh=mesh,
        in_specs=placed,
        out_specs=P(("grp", "pix", "pat"), "ori"),
        check_vma=False,
    )
```

profile of v0, /device:TPU:0, one launch (start us, length us, event | category | flops | bytes accessed | tf_op | source)
XLA Modules:
  0.0 308.1 jit_solution(14089476186193129577)
XLA Ops:
  6.5 0.0 reduce-scatter.3.cloned.1.call-start
  6.5 0.8 select_reduce_fusion.1
  7.3 19.1 %multiply_reduce_fusion = f32[1024]{0:T(1024)S(1)} fusion(bf16[16384,1024]{1,0:T(8,128)(2,1)} %param.7), kind=kLoop, calls=%fused_computation | loop fusion | flops 50330624 | bytes 33558528 | tf_op jit(solution)/shard_map/reduce_sum | solution.py:32
  26.4 0.0 copy-start
  26.4 0.0 copy-start.1
  26.4 27.0 %subtract_multiply_fusion = f32[512,1024]{1,0:T(8,128)} fusion(bf16[512,16384]{1,0:T(8,128)(2,1)} %param.6, bf16[16384,1024]{1,0:T(8,128)(2,1)} %param.7, f32[1024]{0:T(1024)S(1)} %multiply_reduce_fusion, f32[512]{0:T(512)S(1)} %multiply_multiply_fusion, f32[512]{0:T(512)S(1)} %select_reduce_fusion.1), kind=kOutput, calls=%fused_computation.3 | convolution fusion | flops 17181966336 | bytes 52436992 | tf_op jit(solution)/shard_map/dot_general | solution.py:31
  53.4 0.0 reduce-scatter.3.cloned.1.call-update
  53.5 0.0 all-gather.2.cloned.1.call-start
  53.5 0.1 fusion
  53.6 0.0 copy-done
  53.6 0.0 copy-done.1
  53.6 0.1 select_reduce_fusion
  53.7 46.5 %reduce-scatter.3.cloned.1.call-done = f32[128,1024]{1,0:T(8,128)} async-done(((f32[512,1024]{1,0:T(8,128)}), f32[128,1024]{1,0:T(8,128)}) %reduce-scatter.3.cloned.1.call-update) | async-done | bytes 524304 | tf_op jit(solution)/shard_map/reduce_scatter | solution.py:35
  100.2 1.2 add_reduce_fusion
  101.3 4.9 %pmax.7 = f32[128]{0:T(128)S(1)} all-reduce(f32[128]{0:T(128)S(1)} %add_reduce_fusion), channel_id=1, replica_groups=mesh['grp'=2,'pix'=4,'ori'=2,'pat'=2] {'ori'}, use_global_device_ids=true, to_apply=%region_5.6 | all-reduce | flops 128 | bytes 1024 | tf_op jit(solution)/shard_map/pmax | solution.py:19
  106.3 1.3 exponential_reduce_fusion
  107.5 4.9 %psum.14 = f32[128]{0:T(128)S(1)} all-reduce(f32[128]{0:T(128)S(1)} %exponential_reduce_fusion), channel_id=1, replica_groups=mesh['grp'=2,'pix'=4,'ori'=2,'pat'=2] {'ori'}, use_global_device_ids=true, to_apply=%region_7.8 | all-reduce | flops 128 | bytes 1024 | tf_op jit(solution)/shard_map/psum | solution.py:20
  112.5 1.9 multiply_reduce_fusion.1
  114.4 0.0 all-gather.2.cloned.1.call-update
  114.5 0.0 reduce-scatter.5.cloned.1.call-start
  114.5 27.4 %all-gather.2.cloned.1.call-done = bf16[512,1024]{1,0:T(8,128)(2,1)} async-done(((bf16[128,1024]{1,0:T(8,128)(2,1)}), bf16[512,1024]{1,0:T(8,128)(2,1)}) %all-gather.2.cloned.1.call-update) | async-done | bytes 1048592 | tf_op jit(solution)/shard_map/all_gather | solution.py:40
  141.9 32.5 %convolution_bitcast_fusion = f32[16384,1024]{0,1:T(8,128)} fusion(bf16[512,1024]{1,0:T(8,128)(2,1)} %all-gather.2.cloned.1.call-done, bf16[512,16384]{1,0:T(8,128)(2,1)} %param.6), kind=kOutput, calls=%fused_computation.1 | convolution fusion | flops 17179869184 | bytes 84934656 | tf_op jit(solution)/shard_map/dot_general | solution.py:43
  174.4 0.0 reduce-scatter.5.cloned.1.call-update
  174.4 15.0 %constant_dynamic-slice_fusion = bf16[8192,1024]{1,0:T(8,128)(2,1)} fusion(bf16[16384,1024]{1,0:T(8,128)(2,1)} %param.7, s32[]{:T(128)S(6)} %select_n.17), kind=kLoop, calls=%fused_computation.16 | loop fusion | bytes 33554436 | tf_op jit(solution)/shard_map/dynamic_slice | solution.py:50
  189.4 23.3 %copy.11 = bf16[8192,1024]{0,1:T(8,128)(2,1)} copy(bf16[8192,1024]{1,0:T(8,128)(2,1)} %constant_dynamic-slice_fusion) | data formatting | bytes 33554432
  212.7 14.6 %psum.15 = f32[1024]{0:T(1024)S(1)} all-reduce(f32[1024]{0:T(1024)S(1)} %get-tuple-element.7), channel_id=1, replica_groups=mesh['grp'=2,'pix'=4,'ori'=2,'pat'=2] {'pix','pat'}, use_global_device_ids=true, to_apply=%region_10.11 | all-reduce | flops 1024 | bytes 8192 | tf_op jit(solution)/shard_map/psum | solution.py:39
  227.3 29.8 %reduce-scatter.5.cloned.1.call-done = f32[8192,1024]{0,1:T(8,128)} async-done(((f32[16384,1024]{0,1:T(8,128)}), f32[8192,1024]{0,1:T(8,128)}) %reduce-scatter.5.cloned.1.call-update) | async-done | bytes 33554448 | tf_op jit(solution)/shard_map/reduce_scatter | solution.py:42
  257.0 22.1 %divide_convert_fusion = bf16[8192,1024]{0,1:T(8,128)(2,1)} fusion(f32[8192,1024]{0,1:T(8,128)} %reduce-scatter.5.cloned.1.call-done, bf16[8192,1024]{0,1:T(8,128)(2,1)} %copy.11, f32[1024]{0:T(1024)S(1)} %broadcast_add_fusion), kind=kLoop, calls=%fused_computation.2 | loop fusion | flops 41943040 | bytes 67112960 | tf_op jit(solution)/shard_map/convert_element_type | solution.py:52
  279.2 22.4 %copy.10 = bf16[8192,1024]{1,0:T(8,128)(2,1)} copy(bf16[8192,1024]{0,1:T(8,128)(2,1)} %divide_convert_fusion) | data formatting | bytes 33554432 | tf_op jit(solution)/shard_map/convert_element_type | solution.py:52
  (3 shorter events, 0.0 us)
Async XLA Ops:
  6.5 93.6 %reduce-scatter.3.cloned.1.call-start = ((), (), s32[]{:S(2)}) async-start(), calls=%async_computation.2 | async-start | bytes 2621440 | tf_op jit(solution)/shard_map/reduce_scatter | solution.py:35
  26.4 27.2 %copy-start = (s32[1024]{0:T(1024)S(1)}, s32[1024]{0:T(1024)}, u32[]{:S(2)}) copy-start(s32[1024]{0:T(1024)} %param.11) | copy-start | bytes 12292
  26.4 27.2 %copy-start.1 = (f32[8]{0:T(128)S(1)}, f32[8]{0:T(128)}, u32[]{:S(2)}) copy-start(f32[8]{0:T(128)} %param.10) | copy-start | bytes 100
  53.5 88.4 %all-gather.2.cloned.1.call-start = ((), (), s32[]{:S(2)}) async-start(), calls=%async_computation.3 | async-start | bytes 1310720 | tf_op jit(solution)/shard_map/all_gather | solution.py:40
  114.5 142.6 %reduce-scatter.5.cloned.1.call-start = ((), (), s32[]{:S(2)}) async-start(), calls=%async_computation.4 | async-start | bytes 100663296 | tf_op jit(solution)/shard_map/reduce_scatter | solution.py:42
Sparse Core Ops, SparseCore 0:
  53.6 46.5 reduce-scatter.2
  114.6 27.2 all-gather.1
  174.5 82.4 reduce-scatter.4
where the time goes:
time: 310 us; the launch traced here: 308 us
  waiting for transfers between devices  104 us (34%)
  local copies, waits for them, and re-layouts  60.6 us (20%)
  matrix products  59.5 us (19%)
  other arithmetic  46.5 us (15%)
  blocking collectives  24.5 us (8%)
  between operations  13.1 us (4%)
    reduce_scatter x1, waiting for transfers between devices, local(): lax.psum_scatter(partial_term, 'pix', scatter_dimension=0, tiled=True)  46.5 us
    dot_general x1, matrix products, local(): lax.dot_general(patterns, weights, (((0,), (0,)), ((), ())), preferred_el...  32.5 us
    reduce_scatter x1, waiting for transfers between devices, local(): lax.psum_scatter(lax.dot_general(patterns, weights, (((0,), (0,)), ((), (...  29.8 us
    all_gather x1, waiting for transfers between devices, local(): weights = lax.all_gather(weights, 'pix', axis=0, tiled=True)  27.4 us
    dot_general x1, matrix products, local(): cross = jnp.dot(patterns, model, preferred_element_type=jnp.float32)  27 us
    unnamed x5, local copies, waits for them, and re-layouts  23.3 us
    convert_element_type x1, local copies, waits for them, and re-layouts, local(): return (numer / den[None, :]).astype(jnp.bfloat16)  22.4 us
    convert_element_type x1, other arithmetic, local(): return (numer / den[None, :]).astype(jnp.bfloat16)  22.1 us
  transfers between devices with their start and end apart: 3, of which 3 were waited for; matrix products, arithmetic and copies ran while one was open for 12% of the time, Pallas kernels for 0%

commit v1 on v0

v1 whole, which is shorter than its diff:
```python
import functools

import jax
import jax.numpy as jnp
from jax import lax
from jax.experimental import pallas as pl
from jax.experimental.pallas import tpu as pltpu
from jax.sharding import PartitionSpec as P

prior_weight = 0.5
MESH = pl.DeviceIdType.MESH
F32 = jnp.float32
BF16 = jnp.bfloat16


def table_lookup(table, index):
    levels = jnp.arange(table.shape[0], dtype=jnp.int32)
    return jnp.sum(jnp.where(index[:, None] == levels[None, :], table[None, :], 0.0), axis=1)


def block_of(size, most):
    block = min(size, most)
    while size % block:
        block //= 2
    return block


def score_kernel(
    n_pix, n_ori, beta, chunks, width, steps, depth, slots,
    pat_hbm, model_hbm, phi_ref, logw_ref,
    w_ref, den_ref, sib_ref,
    pat_v, mbuf, acc, sq, part, rx, sc, st, dpart,
    pat_sem, m_sem, sib_sem, rs_send, rs_recv, st_send, st_recv,
    agz_send, agz_recv, ags_send, ags_recv,
):
    z = lax.axis_index("pix")
    core = lax.axis_index("pat")
    ori = lax.axis_index("ori")
    last = n_pix - 1
    half_rows = part.shape[2]
    sub = half_rows // 2
    units = chunks * 2
    hops = (z, last - z)
    nexts = (lax.rem(z + 1, n_pix), lax.rem(z + n_pix - 1, n_pix))

    def model_copy(j):
        c, k = j // steps, j % steps
        return pltpu.make_async_copy(
            model_hbm.at[pl.ds(k * depth, depth), pl.ds(c * width, width)],
            mbuf.at[j % slots], m_sem.at[j % slots])

    def pattern_copy(k):
        cols = pl.ds(k * depth, depth)
        return pltpu.make_async_copy(pat_hbm.at[:, cols], pat_v.at[:, cols], pat_sem.at[k])

    total_steps = chunks * steps
    for k in range(steps):
        pattern_copy(k).start()
        if k < min(slots, total_steps):
            model_copy(k).start()
    for j in range(steps, min(slots, total_steps)):
        model_copy(j).start()

    barrier = pltpu.get_barrier_semaphore()
    for d in range(2):
        @pl.when(hops[d] < last)
        def _():
            pl.semaphore_signal(barrier, inc=1, device_id={"pix": nexts[d]}, device_id_type=MESH)
    pl.semaphore_signal(barrier, inc=1, device_id={"pat": 1 - core}, device_id_type=MESH)
    for k in range(1, n_ori):
        pl.semaphore_signal(
            barrier, inc=1, device_id={"ori": lax.rem(ori + k, n_ori)}, device_id_type=MESH)
    @pl.when(hops[0] * hops[1] == 0)
    def _():
        pl.semaphore_wait(barrier, n_ori + 1)

    @pl.when(hops[0] * hops[1] > 0)
    def _():
        pl.semaphore_wait(barrier, n_ori + 2)

    half_pix = sib_ref.shape[1]
    sib_copy = pltpu.make_async_remote_copy(
        src_ref=pat_hbm.at[:, pl.ds((1 - core) * half_pix, half_pix)], dst_ref=sib_ref,
        send_sem=sib_sem.at[0], recv_sem=sib_sem.at[1],
        device_id={"pat": 1 - core}, device_id_type=MESH)

    def rows_of(s):
        return pl.ds(s * sub, sub)

    def rs_copy(d, u):
        c, s = divmod(u, 2)
        return pltpu.make_async_remote_copy(
            src_ref=part.at[d, c, rows_of(s)], dst_ref=rx.at[d, c, rows_of(s)],
            send_sem=rs_send.at[d, u], recv_sem=rs_recv.at[d, u],
            device_id={"pix": nexts[d]}, device_id_type=MESH)

    def relay(d, u):
        c, s = divmod(u, 2)
        rs_copy(d, u).wait_recv()
        rows = rows_of(s)

        @pl.when(hops[d] < last)
        def _():
            part[d, c, rows] = part[d, c, rows] + rx[d, c, rows]
            rs_copy(d, u).start()

        @pl.when(hops[d] == last)
        def _():
            cols = pl.ds(c * width, width)
            sc[rows, cols] = part[d, c, rows] + rx[d, c, rows] + logw_ref[:, cols]

    def early(h, c):
        return max(0, min(2 * (c - h) + 1, units)) if 1 <= c < chunks - 1 else 0

    for c in range(chunks):
        acc[...] = jnp.zeros_like(acc)
        sq[...] = jnp.zeros_like(sq)

        def body(k, carry):
            j = c * steps + k
            slot = j % slots
            if c == 0:
                pattern_copy(k).wait()
            model_copy(j).wait()
            cols = pl.ds(pl.multiple_of(k * depth, depth), depth)
            block = mbuf[slot]
            acc[...] += jnp.dot(pat_v[:, cols], block, preferred_element_type=F32)
            wide = block.astype(F32)
            sq[...] += jnp.sum(wide * wide, axis=0, keepdims=True)

            @pl.when(j + slots < total_steps)
            def _():
                model_copy(j + slots).start()
            return carry

        lax.fori_loop(0, steps, body, 0)
        if c == 0:
            sib_copy.start()
        for d in range(2):
            rows = pl.ds(d * half_rows, half_rows)
            phi = phi_ref[rows, 0:1]
            part[d, c] = beta * (phi * acc[rows] - (0.5 * phi * phi) * sq[...])

            @pl.when(hops[d] == 0)
            def _():
                rs_copy(d, 2 * c).start()
                rs_copy(d, 2 * c + 1).start()

        for h in range(1, last):
            for u in range(early(h, c - 1), early(h, c)):
                for d in range(2):
                    @pl.when(hops[d] == h)
                    def _():
                        relay(d, u)

    done = [early(h, chunks - 2) for h in range(last)]
    for u in range(units):
        skipped = [h for h in range(1, last) if u < done[h]]
        for d in range(2):
            @pl.when(hops[d] > len(skipped))
            def _():
                relay(d, u)

    def weight_block(g, u):
        c, s = divmod(u, 2)
        return pl.ds((1 - g) * half_rows + s * sub, sub), pl.ds(c * width, width)

    def agz_copy(g, u):
        if u < units:
            rows, cols = weight_block(g, u)
            ref = w_ref.at[0, rows, cols]
        else:
            ref = dpart.at[0, g]
        return pltpu.make_async_remote_copy(
            src_ref=ref, dst_ref=ref, send_sem=agz_send.at[g, u], recv_sem=agz_recv.at[g, u],
            device_id={"pix": nexts[g]}, device_id_type=MESH)

    def ags_copy(g, u):
        if u < units:
            rows, cols = weight_block(g, u)
            src, dst = w_ref.at[0, rows, cols], w_ref.at[1, rows, cols]
        else:
            src, dst = dpart.at[0, g], dpart.at[1, g]
        return pltpu.make_async_remote_copy(
            src_ref=src, dst_ref=dst, send_sem=ags_send.at[g, u], recv_sem=ags_recv.at[g, u],
            device_id={"pat": 1 - core}, device_id_type=MESH)

    def st_copy(k):
        return pltpu.make_async_remote_copy(
            src_ref=st.at[0], dst_ref=st.at[k], send_sem=st_send.at[k], recv_sem=st_recv.at[k],
            device_id={"ori": lax.rem(ori + k, n_ori)}, device_id_type=MESH)

    for g in range(2):
        @pl.when(hops[g] == 0)
        def _():
            top = jnp.max(sc[...], axis=1, keepdims=True)
            total = jnp.sum(jnp.exp(sc[...] - top), axis=1, keepdims=True)
            lane = lax.broadcasted_iota(jnp.int32, (half_rows, 128), 1)
            packed = jnp.where(lane == 0, top, jnp.where(lane == 1, total, 0.0))
            st[0] = packed.T[0:8, :]
            for k in range(1, n_ori):
                st_copy(k).start()
            tops, totals = [top], [total]
            for k in range(1, n_ori):
                st_copy(k).wait_recv()
                other = jnp.concatenate(
                    [st[k], jnp.zeros((120, half_rows), F32)], axis=0).T
                tops.append(other[:, 0:1])
                totals.append(other[:, 1:2])
            most = functools.reduce(jnp.maximum, tops)
            whole = sum(t * jnp.exp(m - most) for m, t in zip(tops, totals))
            lse = most + jnp.log(whole)
            phi = phi_ref[(1 - g) * half_rows:(2 - g) * half_rows, 0:1]
            for c in range(chunks):
                cols = slice(c * width, (c + 1) * width)
                prob = jnp.exp(sc[:, cols] - lse)
                w_ref[0, (1 - g) * half_rows:(2 - g) * half_rows, cols] = (prob * phi).astype(BF16)
                dpart[0, g, :, cols] = jnp.sum(prob * (phi * phi), axis=0, keepdims=True)
                for u in (2 * c, 2 * c + 1):
                    agz_copy(g, u).start()
                    ags_copy(g, u).start()
            agz_copy(g, units).start()
            ags_copy(g, units).start()
            for k in range(1, n_ori):
                st_copy(k).wait_send()

    for u in range(units + 1):
        for g in range(2):
            @pl.when(hops[g] > 0)
            def _():
                agz_copy(g, u).wait_recv()

                @pl.when(hops[g] < last)
                def _():
                    agz_copy(g, u).start()
                ags_copy(g, u).start()

    for u in range(units + 1):
        for g in range(2):
            ags_copy(g, u).wait_recv()
    den_ref[...] = prior_weight + (
        (dpart[0, 0] + dpart[0, 1]) + (dpart[1, 0] + dpart[1, 1]))

    sib_copy.wait_recv()
    sib_copy.wait_send()
    for g in range(2):
        for u in range(units + 1):
            ags_copy(g, u).wait_send()

        @pl.when(hops[g] < last)
        def _():
            for u in range(units):
                rs_copy(g, u).wait_send()
            for u in range(units + 1):
                agz_copy(g, u).wait_send()


def update_kernel(half_ref, own_ref, sib_ref, w_ref, den_ref, model_ref, out_ref):
    dims = (((0,), (0,)), ((), ()))
    numer = lax.dot_general(own_ref[...], w_ref[0], dims, preferred_element_type=F32)
    numer += lax.dot_general(sib_ref[...], w_ref[1], dims, preferred_element_type=F32)
    numer += prior_weight * model_ref[...].astype(F32)
    out_ref[...] = (numer / den_ref[...]).astype(BF16)


def local(n_pix, n_ori, patterns, model, scale_table, scale_index, weight_table, weight_class):
    rows, pixels = patterns.shape
    columns = model.shape[1]
    half_pix = pixels // 2
    phi = jnp.broadcast_to(table_lookup(scale_table, scale_index)[:, None], (rows, 128))
    logw = table_lookup(weight_table, weight_class)[None, :]
    beta = float(pixels * n_pix) ** (-0.5)
    width = block_of(columns, 256)
    chunks = columns // width
    depth = block_of(pixels, 2048)
    steps = pixels // depth
    slots = min(8, chunks * steps)
    half_rows = rows // 2
    units = chunks * 2
    dma = pltpu.SemaphoreType.DMA
    any_spec = pl.BlockSpec(memory_space=pl.ANY)
    vmem_spec = pl.BlockSpec(memory_space=pltpu.VMEM)
    weights, den, sibling = pl.pallas_call(
        functools.partial(score_kernel, n_pix, n_ori, beta, chunks, width, steps, depth, slots),
        out_shape=(
            jax.ShapeDtypeStruct((2, rows, columns), BF16),
            jax.ShapeDtypeStruct((1, columns), F32),
            jax.ShapeDtypeStruct((rows, half_pix), BF16),
        ),
        in_specs=[any_spec, any_spec, vmem_spec, vmem_spec],
        out_specs=(vmem_spec, vmem_spec, any_spec),
        scratch_shapes=[
            pltpu.VMEM((rows, pixels), BF16),
            pltpu.VMEM((slots, depth, width), BF16),
            pltpu.VMEM((rows, width), F32),
            pltpu.VMEM((1, width), F32),
            pltpu.VMEM((2, chunks, half_rows, width), F32),
            pltpu.VMEM((2, chunks, half_rows, width), F32),
            pltpu.VMEM((half_rows, columns), F32),
            pltpu.VMEM((n_ori, 8, half_rows), F32),
            pltpu.VMEM((2, 2, 1, columns), F32),
            dma((steps,)),
            dma((slots,)),
            dma((2,)),
            dma((2, units)),
            dma((2, units)),
            dma((n_ori,)),
            dma((n_ori,)),
            dma((2, units + 1)),
            dma((2, units + 1)),
            dma((2, units + 1)),
            dma((2, units + 1)),
        ],
        compiler_params=pltpu.CompilerParams(
            collective_id=0, has_side_effects=True, vmem_limit_bytes=56 * 2**20),
        cost_estimate=pl.CostEstimate(
            flops=2 * rows * pixels * columns,
            bytes_accessed=2 * pixels * (rows + columns), transcendentals=rows * columns),
    )(patterns, model, phi, logw)

    block = block_of(half_pix, 512)
    blocks = half_pix // block
    own_half = lax.axis_index("pat").astype(jnp.int32).reshape(1)
    return pl.pallas_call(
        update_kernel,
        out_shape=jax.ShapeDtypeStruct((half_pix, columns), BF16),
        grid_spec=pltpu.PrefetchScalarGridSpec(
            num_scalar_prefetch=1,
            grid=(blocks,),
            in_specs=[
                pl.BlockSpec((rows, block), lambda i, half: (0, half[0] * blocks + i)),
                pl.BlockSpec((rows, block), lambda i, half: (0, i)),
                pl.BlockSpec((2, rows, columns), lambda i, half: (0, 0, 0)),
                pl.BlockSpec((1, columns), lambda i, half: (0, 0)),
                pl.BlockSpec((block, columns), lambda i, half: (half[0] * blocks + i, 0)),
            ],
            out_specs=pl.BlockSpec((block, columns), lambda i, half: (i, 0)),
        ),
        compiler_params=pltpu.CompilerParams(vmem_limit_bytes=48 * 2**20),
        cost_estimate=pl.CostEstimate(
            flops=4 * rows * half_pix * columns,
            bytes_accessed=4 * half_pix * (rows + columns), transcendentals=0),
    )(own_half, patterns, sibling, weights, den, model)


def solution(mesh):
    placed = (
        P(("grp", "pat"), "pix"),
        P(("grp", "pix"), "ori"),
        P("grp"),
        P(("grp", "pat")),
        P("grp"),
        P(("grp", "ori")),
    )
    return jax.shard_map(
        functools.partial(local, mesh.shape["pix"], mesh.shape["ori"]),
        mesh=mesh,
        in_specs=placed,
        out_specs=P(("grp", "pix", "pat"), "ori"),
        check_vma=False,
    )
```

time: 310 us -> 184 us (0.59)
  Pallas kernels: 0 us -> 178 us
  waiting for transfers between devices: 104 us -> 0 us
  matrix products: 59.5 us -> 0 us
  local copies, waits for them, and re-layouts: 60.6 us -> 3.1 us
  other arithmetic: 46.5 us -> 2.15 us
  blocking collectives: 24.5 us -> 0 us
  between operations: 13.1 us -> 0.02 us
    pallas_call x0 -> x2, Pallas kernels: none -> 178 us  [the longest x1 150 us: local(): pl.pallas_call(functools.partial(score_kernel, n_pix, n_ori, beta, chunks...]
    reduce_scatter x2 -> x0, waiting for transfers between devices: 76.3 us -> none  [the longest x1 46.5 us: local(): lax.psum_scatter(partial_term, 'pix', scatter_dimension=0, tiled=True)]
    dot_general x2 -> x0, matrix products: 59.5 us -> none  [the longest x1 32.5 us: local(): lax.dot_general(patterns, weights, (((0,), (0,)), ((), ())), preferred_el...]
    all_gather x1 -> x0, waiting for transfers between devices: 27.4 us -> none  [local(): weights = lax.all_gather(weights, 'pix', axis=0, tiled=True)]
    convert_element_type x1 -> x0, local copies, waits for them, and re-layouts: 22.4 us -> none  [local(): return (numer / den[None, :]).astype(jnp.bfloat16)]
    reduce_sum x3 -> x0, other arithmetic: 22.3 us -> none  [the longest x1 19.1 us: local(): squares = jnp.sum(jnp.square(model.astype(jnp.float32)), axis=0)]
    convert_element_type x1 -> x0, other arithmetic: 22.1 us -> none  [local(): return (numer / den[None, :]).astype(jnp.bfloat16)]
    unnamed x5 -> x4, local copies, waits for them, and re-layouts: 23.3 us -> 2.27 us
  transfers between devices with their start and end apart: 3 -> 0, of which waited for: 3 -> 0; matrix products, arithmetic and copies ran while one was open for 12% -> 0% of each run, Pallas kernels for 0% -> 0%
where the time goes in v1:
time: 184 us; the launch traced here: 183 us
  Pallas kernels  178 us (97%)
  local copies, waits for them, and re-layouts  3.1 us (2%)
  other arithmetic  2.15 us (1%)
    pallas_call x1, Pallas kernels, local(): pl.pallas_call(functools.partial(score_kernel, n_pix, n_ori, beta, chunks...  150 us
    pallas_call x1, Pallas kernels, local(): pl.pallas_call(update_kernel, out_shape=jax.ShapeDtypeStruct((half_pix, c...  28.4 us

profile of v1, /device:TPU:0, one launch (start us, length us, event | category | flops | bytes accessed | tf_op | source)
XLA Modules:
  0.0 183.3 jit_solution(15338813483475093535)
XLA Ops:
  0.0 0.8 select_reduce_fusion.1
  0.8 1.4 select_reduce_fusion
  2.2 0.8 broadcast_in_dim.41.phi_ref
  3.0 149.6 %shard_map.64 = (bf16[2,512,1024]{2,1,0:T(8,128)(2,1)}, f32[1,1024]{1,0:T(1,128)}, bf16[512,8192]{1,0:T(8,128)(2,1)}) custom-call(bf16[512,16384]{1,0:T(8,128)(2,1)} %own_ref.1, bf16[16384,1024]{1,0:T(8,128)(2,1)} %model_ref.1, f32[512,128]{1,0:T(8,128)} %broadcast_in_dim.41.phi_ref, f32[1,1024]{1,0:T(1,128)} %bitcast.2), custom_call_target="tpu_custom_call" | custom-call | flops 17179869184 | bytes 50331648 | tf_op jit(solution)/shard_map/pallas_call | solution.py:283
  152.6 0.0 copy-start
  152.6 1.6 copy-done
  154.2 0.0 copy-start.1
  154.2 0.7 copy-done.1
  154.9 28.4 %shard_map.65 = bf16[8192,1024]{1,0:T(8,128)(2,1)} custom-call(s32[1]{0:T(128)} %bitcast.half_ref, bf16[512,16384]{1,0:T(8,128)(2,1)} %own_ref.1, bf16[512,8192]{1,0:T(8,128)(2,1)} %get-tuple-element.8.sib_ref, bf16[2,512,1024]{2,1,0:T(8,128)(2,1)S(1)} %copy-done, f32[1,1024]{1,0:T(1,128)S(1)} %copy-done.1, bf16[16384,1024]{1,0:T(8,128)(2,1)} %model_ref.1), custom_call_target="tpu_custom_call" | custom-call | flops 17179869184 | bytes 50331648 | tf_op jit(solution)/shard_map/pallas_call | solution.py:324
Async XLA Ops:
  152.6 1.6 copy-start
  154.2 0.7 copy-start.1

commit v2 on v1

--- a/solution.py
+++ b/solution.py
@@ -26,7 +26,7 @@
 
 
 def score_kernel(
-    n_pix, n_ori, beta, chunks, width, steps, depth, slots,
+    n_pix, n_ori, beta, chunks, subs, width, steps, depth, slots,
     pat_hbm, model_hbm, phi_ref, logw_ref,
     w_ref, den_ref, sib_ref,
     pat_v, mbuf, acc, sq, part, rx, sc, st, dpart,
@@ -38,8 +38,8 @@
     ori = lax.axis_index("ori")
     last = n_pix - 1
     half_rows = part.shape[2]
-    sub = half_rows // 2
-    units = chunks * 2
+    sub = half_rows // subs
+    units = chunks * subs
     hops = (z, last - z)
     nexts = (lax.rem(z + 1, n_pix), lax.rem(z + n_pix - 1, n_pix))
 
@@ -79,23 +79,28 @@
         pl.semaphore_wait(barrier, n_ori + 2)
 
     half_pix = sib_ref.shape[1]
-    sib_copy = pltpu.make_async_remote_copy(
-        src_ref=pat_hbm.at[:, pl.ds((1 - core) * half_pix, half_pix)], dst_ref=sib_ref,
-        send_sem=sib_sem.at[0], recv_sem=sib_sem.at[1],
-        device_id={"pat": 1 - core}, device_id_type=MESH)
+    piece = sib_ref.shape[0] // total_steps
+
+    def sib_copy(j):
+        rows = pl.ds(pl.multiple_of(j * piece, piece), piece)
+        return pltpu.make_async_remote_copy(
+            src_ref=pat_hbm.at[rows, pl.ds((1 - core) * half_pix, half_pix)],
+            dst_ref=sib_ref.at[rows],
+            send_sem=sib_sem.at[0, j], recv_sem=sib_sem.at[1, j],
+            device_id={"pat": 1 - core}, device_id_type=MESH)
 
     def rows_of(s):
         return pl.ds(s * sub, sub)
 
     def rs_copy(d, u):
-        c, s = divmod(u, 2)
+        c, s = divmod(u, subs)
         return pltpu.make_async_remote_copy(
             src_ref=part.at[d, c, rows_of(s)], dst_ref=rx.at[d, c, rows_of(s)],
             send_sem=rs_send.at[d, u], recv_sem=rs_recv.at[d, u],
             device_id={"pix": nexts[d]}, device_id_type=MESH)
 
     def relay(d, u):
-        c, s = divmod(u, 2)
+        c, s = divmod(u, subs)
         rs_copy(d, u).wait_recv()
         rows = rows_of(s)
 
@@ -109,8 +114,10 @@
             cols = pl.ds(c * width, width)
             sc[rows, cols] = part[d, c, rows] + rx[d, c, rows] + logw_ref[:, cols]
 
-    def early(h, c):
-        return max(0, min(2 * (c - h) + 1, units)) if 1 <= c < chunks - 1 else 0
+    marks = []
+    if chunks > 1 and steps >= 8 and last > 2 and subs > 1:
+        marks = [(steps // 2, ((1, 0),)), (steps - 1, ((1, 1), (2, 0)))]
+    relayed = {pair for _, pairs in marks for pair in pairs}
 
     for c in range(chunks):
         acc[...] = jnp.zeros_like(acc)
@@ -131,11 +138,18 @@
             @pl.when(j + slots < total_steps)
             def _():
                 model_copy(j + slots).start()
+            sib_copy(j).start()
             return carry
 
-        lax.fori_loop(0, steps, body, 0)
-        if c == 0:
-            sib_copy.start()
+        start = 0
+        for stop, pairs in (marks if c == chunks - 1 else []) + [(steps, ())]:
+            lax.fori_loop(start, stop, body, 0)
+            start = stop
+            for h, u in pairs:
+                for d in range(2):
+                    @pl.when(hops[d] == h)
+                    def _():
+                        relay(d, u)
         for d in range(2):
             rows = pl.ds(d * half_rows, half_rows)
             phi = phi_ref[rows, 0:1]
@@ -143,26 +157,18 @@
 
             @pl.when(hops[d] == 0)
             def _():
-                rs_copy(d, 2 * c).start()
-                rs_copy(d, 2 * c + 1).start()
-
-        for h in range(1, last):
-            for u in range(early(h, c - 1), early(h, c)):
-                for d in range(2):
-                    @pl.when(hops[d] == h)
-                    def _():
-                        relay(d, u)
-
-    done = [early(h, chunks - 2) for h in range(last)]
+                for u in range(c * subs, (c + 1) * subs):
+                    rs_copy(d, u).start()
+
     for u in range(units):
-        skipped = [h for h in range(1, last) if u < done[h]]
+        skipped = sum((h, u) in relayed for h in range(1, last))
         for d in range(2):
-            @pl.when(hops[d] > len(skipped))
+            @pl.when(hops[d] > skipped)
             def _():
                 relay(d, u)
 
     def weight_block(g, u):
-        c, s = divmod(u, 2)
+        c, s = divmod(u, subs)
         return pl.ds((1 - g) * half_rows + s * sub, sub), pl.ds(c * width, width)
 
     def agz_copy(g, u):
@@ -216,7 +222,7 @@
                 prob = jnp.exp(sc[:, cols] - lse)
                 w_ref[0, (1 - g) * half_rows:(2 - g) * half_rows, cols] = (prob * phi).astype(BF16)
                 dpart[0, g, :, cols] = jnp.sum(prob * (phi * phi), axis=0, keepdims=True)
-                for u in (2 * c, 2 * c + 1):
+                for u in range(c * subs, (c + 1) * subs):
                     agz_copy(g, u).start()
                     ags_copy(g, u).start()
             agz_copy(g, units).start()
@@ -238,11 +244,15 @@
     for u in range(units + 1):
         for g in range(2):
             ags_copy(g, u).wait_recv()
-    den_ref[...] = prior_weight + (
-        (dpart[0, 0] + dpart[0, 1]) + (dpart[1, 0] + dpart[1, 1]))
-
-    sib_copy.wait_recv()
-    sib_copy.wait_send()
+    den_ref[...] = 1.0 / (prior_weight + (
+        (dpart[0, 0] + dpart[0, 1]) + (dpart[1, 0] + dpart[1, 1])))
+
+    def settle(j, carry):
+        sib_copy(j).wait_recv()
+        sib_copy(j).wait_send()
+        return carry
+
+    lax.fori_loop(0, total_steps, settle, 0)
     for g in range(2):
         for u in range(units + 1):
             ags_copy(g, u).wait_send()
@@ -255,12 +265,15 @@
                 agz_copy(g, u).wait_send()
 
 
-def update_kernel(half_ref, own_ref, sib_ref, w_ref, den_ref, model_ref, out_ref):
-    dims = (((0,), (0,)), ((), ()))
-    numer = lax.dot_general(own_ref[...], w_ref[0], dims, preferred_element_type=F32)
-    numer += lax.dot_general(sib_ref[...], w_ref[1], dims, preferred_element_type=F32)
-    numer += prior_weight * model_ref[...].astype(F32)
-    out_ref[...] = (numer / den_ref[...]).astype(BF16)
+def update_kernel(width, half_ref, own_ref, sib_ref, w_ref, inverse_ref, model_ref, out_ref):
+    pats = jnp.concatenate([own_ref[...].T, sib_ref[...].T], axis=1)
+    both, rows, columns = w_ref.shape
+    for c in range(columns // width):
+        cols = slice(c * width, (c + 1) * width)
+        weights = w_ref[:, :, cols].reshape(both * rows, width)
+        numer = jnp.dot(pats, weights, preferred_element_type=F32)
+        numer += prior_weight * model_ref[:, cols].astype(F32)
+        out_ref[:, cols] = (numer * inverse_ref[:, cols]).astype(BF16)
 
 
 def local(n_pix, n_ori, patterns, model, scale_table, scale_index, weight_table, weight_class):
@@ -270,18 +283,19 @@
     phi = jnp.broadcast_to(table_lookup(scale_table, scale_index)[:, None], (rows, 128))
     logw = table_lookup(weight_table, weight_class)[None, :]
     beta = float(pixels * n_pix) ** (-0.5)
-    width = block_of(columns, 256)
+    width = block_of(columns, 512)
     chunks = columns // width
     depth = block_of(pixels, 2048)
     steps = pixels // depth
     slots = min(8, chunks * steps)
     half_rows = rows // 2
-    units = chunks * 2
+    subs = 4
+    units = chunks * subs
     dma = pltpu.SemaphoreType.DMA
     any_spec = pl.BlockSpec(memory_space=pl.ANY)
     vmem_spec = pl.BlockSpec(memory_space=pltpu.VMEM)
-    weights, den, sibling = pl.pallas_call(
-        functools.partial(score_kernel, n_pix, n_ori, beta, chunks, width, steps, depth, slots),
+    weights, inverse, sibling = pl.pallas_call(
+        functools.partial(score_kernel, n_pix, n_ori, beta, chunks, subs, width, steps, depth, slots),
         out_shape=(
             jax.ShapeDtypeStruct((2, rows, columns), BF16),
             jax.ShapeDtypeStruct((1, columns), F32),
@@ -301,7 +315,7 @@
             pltpu.VMEM((2, 2, 1, columns), F32),
             dma((steps,)),
             dma((slots,)),
-            dma((2,)),
+            dma((2, chunks * steps)),
             dma((2, units)),
             dma((2, units)),
             dma((n_ori,)),
@@ -322,7 +336,7 @@
     blocks = half_pix // block
     own_half = lax.axis_index("pat").astype(jnp.int32).reshape(1)
     return pl.pallas_call(
-        update_kernel,
+        functools.partial(update_kernel, block_of(columns, 256)),
         out_shape=jax.ShapeDtypeStruct((half_pix, columns), BF16),
         grid_spec=pltpu.PrefetchScalarGridSpec(
             num_scalar_prefetch=1,
@@ -336,11 +350,11 @@
             ],
             out_specs=pl.BlockSpec((block, columns), lambda i, half: (i, 0)),
         ),
-        compiler_params=pltpu.CompilerParams(vmem_limit_bytes=48 * 2**20),
+        compiler_params=pltpu.CompilerParams(vmem_limit_bytes=60 * 2**20),
         cost_estimate=pl.CostEstimate(
             flops=4 * rows * half_pix * columns,
             bytes_accessed=4 * half_pix * (rows + columns), transcendentals=0),
-    )(own_half, patterns, sibling, weights, den, model)
+    )(own_half, patterns, sibling, weights, inverse, model)
 
 
 def solution(mesh):

time: 184 us -> 189 us (1.027)
  Pallas kernels: 178 us -> 185 us
  local copies, waits for them, and re-layouts: 3.1 us -> 0.84 us
    pallas_call x1, Pallas kernels: 150 us -> 156 us  [local(): pl.pallas_call(functools.partial(score_kernel, n_pix, n_ori, beta, chunks...]
    unnamed x4 -> x0, local copies, waits for them, and re-layouts: 2.27 us -> none
where the time goes in v2:
time: 189 us; the launch traced here: 188 us
  Pallas kernels  185 us (98%)
  other arithmetic  2.16 us (1%)
    pallas_call x1, Pallas kernels, local(): pl.pallas_call(functools.partial(score_kernel, n_pix, n_ori, beta, chunks...  156 us
    pallas_call x1, Pallas kernels, local(): pl.pallas_call(functools.partial(update_kernel, block_of(columns, 256)),...  29.3 us

profile of v2, /device:TPU:0, one launch (start us, length us, event | category | flops | bytes accessed | tf_op | source)
XLA Modules:
  0.0 188.1 jit_solution(17912355967220469871)
XLA Ops:
  0.0 0.8 select_reduce_fusion.1
  0.8 1.4 select_reduce_fusion
  2.2 0.8 broadcast_in_dim.41.phi_ref
  3.0 155.8 %shard_map.64 = (bf16[2,512,1024]{2,1,0:T(8,128)(2,1)}, f32[1,1024]{1,0:T(1,128)}, bf16[512,8192]{1,0:T(8,128)(2,1)}) custom-call(bf16[512,16384]{1,0:T(8,128)(2,1)} %own_ref.1, bf16[16384,1024]{1,0:T(8,128)(2,1)} %model_ref.1, f32[512,128]{1,0:T(8,128)} %broadcast_in_dim.41.phi_ref, f32[1,1024]{1,0:T(1,128)} %bitcast.2), custom_call_target="tpu_custom_call" | custom-call | flops 17179869184 | bytes 50331648 | tf_op jit(solution)/shard_map/pallas_call | solution.py:297
  158.8 29.3 %shard_map.65 = bf16[8192,1024]{1,0:T(8,128)(2,1)} custom-call(s32[1]{0:T(128)} %bitcast.half_ref, bf16[512,16384]{1,0:T(8,128)(2,1)} %own_ref.1, bf16[512,8192]{1,0:T(8,128)(2,1)} %get-tuple-element.8.sib_ref, bf16[2,512,1024]{2,1,0:T(8,128)(2,1)} %get-tuple-element.9.w_ref, f32[1,1024]{1,0:T(1,128)} %get-tuple-element.10.inverse_ref, ...), custom_call_target="tpu_custom_call" | custom-call | flops 17179869184 | bytes 50331648 | tf_op jit(solution)/shard_map/pallas_call | solution.py:338

commit v3 on v2

--- a/solution.py
+++ b/solution.py
@@ -28,9 +28,9 @@
 def score_kernel(
     n_pix, n_ori, beta, chunks, subs, width, steps, depth, slots,
     pat_hbm, model_hbm, phi_ref, logw_ref,
-    w_ref, den_ref, sib_ref,
+    w_ref, den_ref,
     pat_v, mbuf, acc, sq, part, rx, sc, st, dpart,
-    pat_sem, m_sem, sib_sem, rs_send, rs_recv, st_send, st_recv,
+    pat_sem, m_sem, rs_send, rs_recv, st_send, st_recv,
     agz_send, agz_recv, ags_send, ags_recv,
 ):
     z = lax.axis_index("pix")
@@ -54,6 +54,7 @@
         return pltpu.make_async_copy(pat_hbm.at[:, cols], pat_v.at[:, cols], pat_sem.at[k])
 
     total_steps = chunks * steps
+    fine = block_of(depth, 512)
     for k in range(steps):
         pattern_copy(k).start()
         if k < min(slots, total_steps):
@@ -78,17 +79,6 @@
     def _():
         pl.semaphore_wait(barrier, n_ori + 2)
 
-    half_pix = sib_ref.shape[1]
-    piece = sib_ref.shape[0] // total_steps
-
-    def sib_copy(j):
-        rows = pl.ds(pl.multiple_of(j * piece, piece), piece)
-        return pltpu.make_async_remote_copy(
-            src_ref=pat_hbm.at[rows, pl.ds((1 - core) * half_pix, half_pix)],
-            dst_ref=sib_ref.at[rows],
-            send_sem=sib_sem.at[0, j], recv_sem=sib_sem.at[1, j],
-            device_id={"pat": 1 - core}, device_id_type=MESH)
-
     def rows_of(s):
         return pl.ds(s * sub, sub)
 
@@ -129,16 +119,19 @@
             if c == 0:
                 pattern_copy(k).wait()
             model_copy(j).wait()
-            cols = pl.ds(pl.multiple_of(k * depth, depth), depth)
-            block = mbuf[slot]
-            acc[...] += jnp.dot(pat_v[:, cols], block, preferred_element_type=F32)
-            wide = block.astype(F32)
-            sq[...] += jnp.sum(wide * wide, axis=0, keepdims=True)
+            def inner(i, carry):
+                cols = pl.ds(pl.multiple_of(k * depth + i * fine, fine), fine)
+                block = mbuf[slot, pl.ds(pl.multiple_of(i * fine, fine), fine)]
+                acc[...] += jnp.dot(pat_v[:, cols], block, preferred_element_type=F32)
+                wide = block.astype(F32).reshape(fine // 8, 8, width)
+                sq[...] += jnp.sum(wide * wide, axis=0)
+                return carry
+
+            lax.fori_loop(0, depth // fine, inner, 0)
 
             @pl.when(j + slots < total_steps)
             def _():
                 model_copy(j + slots).start()
-            sib_copy(j).start()
             return carry
 
         start = 0
@@ -150,10 +143,11 @@
                     @pl.when(hops[d] == h)
                     def _():
                         relay(d, u)
+        squares = jnp.sum(sq[...], axis=0, keepdims=True)
         for d in range(2):
             rows = pl.ds(d * half_rows, half_rows)
             phi = phi_ref[rows, 0:1]
-            part[d, c] = beta * (phi * acc[rows] - (0.5 * phi * phi) * sq[...])
+            part[d, c] = beta * (phi * acc[rows] - (0.5 * phi * phi) * squares)
 
             @pl.when(hops[d] == 0)
             def _():
@@ -247,12 +241,6 @@
     den_ref[...] = 1.0 / (prior_weight + (
         (dpart[0, 0] + dpart[0, 1]) + (dpart[1, 0] + dpart[1, 1])))
 
-    def settle(j, carry):
-        sib_copy(j).wait_recv()
-        sib_copy(j).wait_send()
-        return carry
-
-    lax.fori_loop(0, total_steps, settle, 0)
     for g in range(2):
         for u in range(units + 1):
             ags_copy(g, u).wait_send()
@@ -265,12 +253,12 @@
                 agz_copy(g, u).wait_send()
 
 
-def update_kernel(width, half_ref, own_ref, sib_ref, w_ref, inverse_ref, model_ref, out_ref):
-    pats = jnp.concatenate([own_ref[...].T, sib_ref[...].T], axis=1)
-    both, rows, columns = w_ref.shape
+def update_kernel(width, place_ref, pat_ref, first_ref, second_ref, inverse_ref, model_ref, out_ref):
+    pats = pat_ref[...].T
+    columns = out_ref.shape[1]
     for c in range(columns // width):
         cols = slice(c * width, (c + 1) * width)
-        weights = w_ref[:, :, cols].reshape(both * rows, width)
+        weights = jnp.concatenate([first_ref[0, :, cols], second_ref[0, :, cols]], axis=0)
         numer = jnp.dot(pats, weights, preferred_element_type=F32)
         numer += prior_weight * model_ref[:, cols].astype(F32)
         out_ref[:, cols] = (numer * inverse_ref[:, cols]).astype(BF16)
@@ -294,20 +282,20 @@
     dma = pltpu.SemaphoreType.DMA
     any_spec = pl.BlockSpec(memory_space=pl.ANY)
     vmem_spec = pl.BlockSpec(memory_space=pltpu.VMEM)
-    weights, inverse, sibling = pl.pallas_call(
+    gathered = lax.all_gather(patterns, "pat", axis=0, tiled=True)
+    weights, inverse = pl.pallas_call(
         functools.partial(score_kernel, n_pix, n_ori, beta, chunks, subs, width, steps, depth, slots),
         out_shape=(
             jax.ShapeDtypeStruct((2, rows, columns), BF16),
             jax.ShapeDtypeStruct((1, columns), F32),
-            jax.ShapeDtypeStruct((rows, half_pix), BF16),
         ),
         in_specs=[any_spec, any_spec, vmem_spec, vmem_spec],
-        out_specs=(vmem_spec, vmem_spec, any_spec),
+        out_specs=(vmem_spec, vmem_spec),
         scratch_shapes=[
             pltpu.VMEM((rows, pixels), BF16),
             pltpu.VMEM((slots, depth, width), BF16),
             pltpu.VMEM((rows, width), F32),
-            pltpu.VMEM((1, width), F32),
+            pltpu.VMEM((8, width), F32),
             pltpu.VMEM((2, chunks, half_rows, width), F32),
             pltpu.VMEM((2, chunks, half_rows, width), F32),
             pltpu.VMEM((half_rows, columns), F32),
@@ -315,7 +303,6 @@
             pltpu.VMEM((2, 2, 1, columns), F32),
             dma((steps,)),
             dma((slots,)),
-            dma((2, chunks * steps)),
             dma((2, units)),
             dma((2, units)),
             dma((n_ori,)),
@@ -342,9 +329,9 @@
             num_scalar_prefetch=1,
             grid=(blocks,),
             in_specs=[
-                pl.BlockSpec((rows, block), lambda i, half: (0, half[0] * blocks + i)),
-                pl.BlockSpec((rows, block), lambda i, half: (0, i)),
-                pl.BlockSpec((2, rows, columns), lambda i, half: (0, 0, 0)),
+                pl.BlockSpec((2 * rows, block), lambda i, half: (0, half[0] * blocks + i)),
+                pl.BlockSpec((1, rows, columns), lambda i, half: (half[0], 0, 0)),
+                pl.BlockSpec((1, rows, columns), lambda i, half: (1 - half[0], 0, 0)),
                 pl.BlockSpec((1, columns), lambda i, half: (0, 0)),
                 pl.BlockSpec((block, columns), lambda i, half: (half[0] * blocks + i, 0)),
             ],
@@ -354,7 +341,7 @@
         cost_estimate=pl.CostEstimate(
             flops=4 * rows * half_pix * columns,
             bytes_accessed=4 * half_pix * (rows + columns), transcendentals=0),
-    )(own_half, patterns, sibling, weights, inverse, model)
+    )(own_half, gathered, weights, weights, inverse, model)
 
 
 def solution(mesh):

time: 189 us -> 209 us (1.11)
  between operations: 0.01 us -> 13.4 us
  Pallas kernels: 185 us -> 192 us
    pallas_call x1, Pallas kernels: 156 us -> 163 us  [local(): pl.pallas_call(functools.partial(score_kernel, n_pix, n_ori, beta, chunks...]
  transfers between devices with their start and end apart: 0 -> 1, of which waited for: 0 -> 0; matrix products, arithmetic and copies ran while one was open for 0% -> 1% of each run, Pallas kernels for 0% -> 78%
where the time goes in v3:
time: 209 us; the launch traced here: 208 us
  Pallas kernels  192 us (92%)
  between operations  13.4 us (6%)
    pallas_call x1, Pallas kernels, local(): pl.pallas_call(functools.partial(score_kernel, n_pix, n_ori, beta, chunks...  163 us
    pallas_call x1, Pallas kernels, local(): pl.pallas_call(functools.partial(update_kernel, block_of(columns, 256)),...  29.1 us
  transfers between devices with their start and end apart: 1, of which 0 were waited for; matrix products, arithmetic and copies ran while one was open for 1% of the time, Pallas kernels for 78%

profile of v3, /device:TPU:0, one launch (start us, length us, event | category | flops | bytes accessed | tf_op | source)
XLA Modules:
  0.0 207.9 jit_solution(12176211919003492307)
XLA Ops:
  6.5 0.0 copy-start.1
  6.5 0.0 copy-start.2
  6.5 0.0 copy-start
  6.5 0.0 copy-start.3
  6.5 0.0 all-gather.2.cloned.1.call-start
  6.6 0.7 all-gather.2.cloned.1.call-update
  7.3 0.0 copy-done.1
  7.3 0.0 copy-done.2
  7.3 0.1 select_reduce_fusion.1
  7.4 0.0 copy-done
  7.4 0.0 copy-done.3
  7.4 0.7 select_reduce_fusion
  8.1 0.8 broadcast_in_dim.41.phi_ref
  8.9 163.0 %shard_map.64 = (bf16[2,512,1024]{2,1,0:T(8,128)(2,1)}, f32[1,1024]{1,0:T(1,128)}) custom-call(bf16[512,16384]{1,0:T(8,128)(2,1)} %pat_hbm.1, bf16[16384,1024]{1,0:T(8,128)(2,1)} %model_ref.1, f32[512,128]{1,0:T(8,128)} %broadcast_in_dim.41.phi_ref, f32[1,1024]{1,0:T(1,128)} %bitcast.2), custom_call_target="tpu_custom_call" | custom-call | flops 17179869184 | bytes 50331648 | tf_op jit(solution)/shard_map/pallas_call | solution.py:286
  171.9 0.0 all-gather.2.cloned.1.call-done.pat_ref
  171.9 29.1 %shard_map.65 = bf16[8192,1024]{1,0:T(8,128)(2,1)} custom-call(s32[1]{0:T(128)} %bitcast.place_ref, bf16[1024,16384]{1,0:T(8,128)(2,1)} %all-gather.2.cloned.1.call-done.pat_ref, bf16[2,512,1024]{2,1,0:T(8,128)(2,1)} %get-tuple-element.7.first_ref.second_ref, bf16[2,512,1024]{2,1,0:T(8,128)(2,1)} %get-tuple-element.7.first_ref.second_ref, ...), custom_call_target="tpu_custom_call" | custom-call | flops 17179869184 | bytes 50331648 | tf_op jit(solution)/shard_map/pallas_call | solution.py:325
Async XLA Ops:
  6.5 0.7 copy-start.1
  6.5 0.8 copy-start.2
  6.5 0.8 copy-start
  6.5 0.8 copy-start.3
  6.5 165.4 %all-gather.2.cloned.1.call-start = ((), (), s32[]{:S(2)}) async-start(), calls=%async_computation | async-start | bytes 50331648 | tf_op jit(solution)/shard_map/all_gather | solution.py:285
Sparse Core Ops, SparseCore 0:
  8.9 53.9 all-gather.1

commit v4 on v3

--- a/solution.py
+++ b/solution.py
@@ -54,7 +54,7 @@
         return pltpu.make_async_copy(pat_hbm.at[:, cols], pat_v.at[:, cols], pat_sem.at[k])
 
     total_steps = chunks * steps
-    fine = block_of(depth, 512)
+    fine = block_of(depth, 2048)
     for k in range(steps):
         pattern_copy(k).start()
         if k < min(slots, total_steps):
@@ -80,17 +80,17 @@
         pl.semaphore_wait(barrier, n_ori + 2)
 
     def rows_of(s):
-        return pl.ds(s * sub, sub)
+        return pl.ds(pl.multiple_of(s * sub, sub), sub)
 
     def rs_copy(d, u):
-        c, s = divmod(u, subs)
+        c, s = u // subs, u % subs
         return pltpu.make_async_remote_copy(
             src_ref=part.at[d, c, rows_of(s)], dst_ref=rx.at[d, c, rows_of(s)],
             send_sem=rs_send.at[d, u], recv_sem=rs_recv.at[d, u],
             device_id={"pix": nexts[d]}, device_id_type=MESH)
 
     def relay(d, u):
-        c, s = divmod(u, subs)
+        c, s = u // subs, u % subs
         rs_copy(d, u).wait_recv()
         rows = rows_of(s)
 
@@ -101,13 +101,20 @@
 
         @pl.when(hops[d] == last)
         def _():
-            cols = pl.ds(c * width, width)
+            cols = pl.ds(pl.multiple_of(c * width, width), width)
             sc[rows, cols] = part[d, c, rows] + rx[d, c, rows] + logw_ref[:, cols]
 
-    marks = []
-    if chunks > 1 and steps >= 8 and last > 2 and subs > 1:
-        marks = [(steps // 2, ((1, 0),)), (steps - 1, ((1, 1), (2, 0)))]
-    relayed = {pair for _, pairs in marks for pair in pairs}
+    def relay_slot(t):
+        for d in range(2):
+            u = t - 2 * (hops[d] - 1)
+
+            @pl.when((hops[d] > 0) & (u >= 0) & (u < units))
+            def _():
+                relay(d, u)
+
+    early = (chunks - 1) * subs
+    if early > steps:
+        early = 0
 
     for c in range(chunks):
         acc[...] = jnp.zeros_like(acc)
@@ -132,17 +139,13 @@
             @pl.when(j + slots < total_steps)
             def _():
                 model_copy(j + slots).start()
+            if early and c == chunks - 1:
+                @pl.when(k >= steps - early)
+                def _():
+                    relay_slot(k - (steps - early))
             return carry
 
-        start = 0
-        for stop, pairs in (marks if c == chunks - 1 else []) + [(steps, ())]:
-            lax.fori_loop(start, stop, body, 0)
-            start = stop
-            for h, u in pairs:
-                for d in range(2):
-                    @pl.when(hops[d] == h)
-                    def _():
-                        relay(d, u)
+        lax.fori_loop(0, steps, body, 0)
         squares = jnp.sum(sq[...], axis=0, keepdims=True)
         for d in range(2):
             rows = pl.ds(d * half_rows, half_rows)
@@ -154,36 +157,39 @@
                 for u in range(c * subs, (c + 1) * subs):
                     rs_copy(d, u).start()
 
-    for u in range(units):
-        skipped = sum((h, u) in relayed for h in range(1, last))
-        for d in range(2):
-            @pl.when(hops[d] > skipped)
-            def _():
-                relay(d, u)
+    def later_slot(t, carry):
+        relay_slot(t)
+        return carry
+
+    lax.fori_loop(early, units + 2 * (last - 1), later_slot, 0)
 
     def weight_block(g, u):
-        c, s = divmod(u, subs)
-        return pl.ds((1 - g) * half_rows + s * sub, sub), pl.ds(c * width, width)
-
-    def agz_copy(g, u):
-        if u < units:
-            rows, cols = weight_block(g, u)
-            ref = w_ref.at[0, rows, cols]
-        else:
-            ref = dpart.at[0, g]
+        c, s = u // subs, u % subs
+        return (pl.ds(pl.multiple_of((1 - g) * half_rows + s * sub, sub), sub),
+                pl.ds(pl.multiple_of(c * width, width), width))
+
+    def agz_copy(g, u, sums=False):
+        rows, cols = weight_block(g, u)
+        ref = dpart.at[0, g] if sums else w_ref.at[0, rows, cols]
         return pltpu.make_async_remote_copy(
             src_ref=ref, dst_ref=ref, send_sem=agz_send.at[g, u], recv_sem=agz_recv.at[g, u],
             device_id={"pix": nexts[g]}, device_id_type=MESH)
 
-    def ags_copy(g, u):
-        if u < units:
-            rows, cols = weight_block(g, u)
-            src, dst = w_ref.at[0, rows, cols], w_ref.at[1, rows, cols]
-        else:
-            src, dst = dpart.at[0, g], dpart.at[1, g]
+    def ags_copy(g, u, sums=False):
+        rows, cols = weight_block(g, u)
+        src = dpart.at[0, g] if sums else w_ref.at[0, rows, cols]
+        dst = dpart.at[1, g] if sums else w_ref.at[1, rows, cols]
         return pltpu.make_async_remote_copy(
             src_ref=src, dst_ref=dst, send_sem=ags_send.at[g, u], recv_sem=ags_recv.at[g, u],
             device_id={"pat": 1 - core}, device_id_type=MESH)
+
+    def forward(g, u, sums=False):
+        agz_copy(g, u, sums).wait_recv()
+
+        @pl.when(hops[g] < last)
+        def _():
+            agz_copy(g, u, sums).start()
+        ags_copy(g, u, sums).start()
 
     def st_copy(k):
         return pltpu.make_async_remote_copy(
@@ -219,38 +225,47 @@
                 for u in range(c * subs, (c + 1) * subs):
                     agz_copy(g, u).start()
                     ags_copy(g, u).start()
-            agz_copy(g, units).start()
-            ags_copy(g, units).start()
+            agz_copy(g, units, True).start()
+            ags_copy(g, units, True).start()
             for k in range(1, n_ori):
                 st_copy(k).wait_send()
 
-    for u in range(units + 1):
+    def gather_slot(t, carry):
         for g in range(2):
-            @pl.when(hops[g] > 0)
-            def _():
-                agz_copy(g, u).wait_recv()
-
-                @pl.when(hops[g] < last)
-                def _():
-                    agz_copy(g, u).start()
-                ags_copy(g, u).start()
-
-    for u in range(units + 1):
-        for g in range(2):
-            ags_copy(g, u).wait_recv()
+            u = t - 2 * (hops[g] - 1)
+
+            @pl.when((hops[g] > 0) & (u >= 0) & (u < units))
+            def _():
+                forward(g, u)
+
+            @pl.when((hops[g] > 0) & (u == units))
+            def _():
+                forward(g, units, True)
+        return carry
+
+    lax.fori_loop(0, units + 1 + 2 * (last - 1), gather_slot, 0)
+
+    def each_unit(action):
+        def step(u, carry):
+            action(u)
+            return carry
+        lax.fori_loop(0, units, step, 0)
+
+    for g in range(2):
+        each_unit(lambda u: ags_copy(g, u).wait_recv())
+        ags_copy(g, units, True).wait_recv()
     den_ref[...] = 1.0 / (prior_weight + (
         (dpart[0, 0] + dpart[0, 1]) + (dpart[1, 0] + dpart[1, 1])))
 
     for g in range(2):
-        for u in range(units + 1):
-            ags_copy(g, u).wait_send()
+        each_unit(lambda u: ags_copy(g, u).wait_send())
+        ags_copy(g, units, True).wait_send()
 
         @pl.when(hops[g] < last)
         def _():
-            for u in range(units):
-                rs_copy(g, u).wait_send()
-            for u in range(units + 1):
-                agz_copy(g, u).wait_send()
+            each_unit(lambda u: rs_copy(g, u).wait_send())
+            each_unit(lambda u: agz_copy(g, u).wait_send())
+            agz_copy(g, units, True).wait_send()
 
 
 def update_kernel(width, place_ref, pat_ref, first_ref, second_ref, inverse_ref, model_ref, out_ref):
@@ -277,7 +292,7 @@
     steps = pixels // depth
     slots = min(8, chunks * steps)
     half_rows = rows // 2
-    subs = 4
+    subs = 8
     units = chunks * subs
     dma = pltpu.SemaphoreType.DMA
     any_spec = pl.BlockSpec(memory_space=pl.ANY)

time: 209 us -> 137 us (0.66)
  Pallas kernels: 192 us -> 121 us
    pallas_call x1, Pallas kernels: 163 us -> 91.5 us  [local(): pl.pallas_call(functools.partial(score_kernel, n_pix, n_ori, beta, chunks...]
  transfers between devices with their start and end apart: 1 -> 1, of which waited for: 0 -> 0; matrix products, arithmetic and copies ran while one was open for 1% -> 1% of each run, Pallas kernels for 78% -> 67%
where the time goes in v4:
time: 137 us; the launch traced here: 136 us
  Pallas kernels  121 us (88%)
  between operations  13.4 us (10%)
    pallas_call x1, Pallas kernels, local(): pl.pallas_call(functools.partial(score_kernel, n_pix, n_ori, beta, chunks...  91.5 us
    pallas_call x1, Pallas kernels, local(): pl.pallas_call(functools.partial(update_kernel, block_of(columns, 256)),...  29.1 us
  transfers between devices with their start and end apart: 1, of which 0 were waited for; matrix products, arithmetic and copies ran while one was open for 1% of the time, Pallas kernels for 67%

profile of v4, /device:TPU:0, one launch (start us, length us, event | category | flops | bytes accessed | tf_op | source)
XLA Modules:
  0.0 136.4 jit_solution(17116560726119116410)
XLA Ops:
  6.5 0.0 copy-start.1
  6.5 0.0 copy-start.2
  6.5 0.0 copy-start
  6.5 0.0 copy-start.3
  6.5 0.0 all-gather.2.cloned.1.call-start
  6.6 0.7 all-gather.2.cloned.1.call-update
  7.3 0.0 copy-done.1
  7.3 0.0 copy-done.2
  7.3 0.1 select_reduce_fusion.1
  7.4 0.0 copy-done
  7.4 0.0 copy-done.3
  7.4 0.7 select_reduce_fusion
  8.1 0.8 broadcast_in_dim.41.phi_ref
  8.9 91.5 %shard_map.64 = (bf16[2,512,1024]{2,1,0:T(8,128)(2,1)}, f32[1,1024]{1,0:T(1,128)}) custom-call(bf16[512,16384]{1,0:T(8,128)(2,1)} %pat_hbm.1, bf16[16384,1024]{1,0:T(8,128)(2,1)} %model_ref.1, f32[512,128]{1,0:T(8,128)} %broadcast_in_dim.41.phi_ref, f32[1,1024]{1,0:T(1,128)} %bitcast.2), custom_call_target="tpu_custom_call" | custom-call | flops 17179869184 | bytes 50331648 | tf_op jit(solution)/shard_map/pallas_call | solution.py:301
  100.4 0.0 all-gather.2.cloned.1.call-done.pat_ref
  100.5 29.1 %shard_map.65 = bf16[8192,1024]{1,0:T(8,128)(2,1)} custom-call(s32[1]{0:T(128)} %bitcast.place_ref, bf16[1024,16384]{1,0:T(8,128)(2,1)} %all-gather.2.cloned.1.call-done.pat_ref, bf16[2,512,1024]{2,1,0:T(8,128)(2,1)} %get-tuple-element.7.first_ref.second_ref, bf16[2,512,1024]{2,1,0:T(8,128)(2,1)} %get-tuple-element.7.first_ref.second_ref, ...), custom_call_target="tpu_custom_call" | custom-call | flops 17179869184 | bytes 50331648 | tf_op jit(solution)/shard_map/pallas_call | solution.py:340
Async XLA Ops:
  6.5 0.7 copy-start.1
  6.5 0.8 copy-start.2
  6.5 0.8 copy-start
  6.5 0.8 copy-start.3
  6.5 93.9 %all-gather.2.cloned.1.call-start = ((), (), s32[]{:S(2)}) async-start(), calls=%async_computation | async-start | bytes 50331648 | tf_op jit(solution)/shard_map/all_gather | solution.py:300
Sparse Core Ops, SparseCore 0:
  8.9 53.9 all-gather.1

commit v5 on v4

--- a/solution.py
+++ b/solution.py
@@ -230,9 +230,11 @@
             for k in range(1, n_ori):
                 st_copy(k).wait_send()
 
+    lag = 4
+
     def gather_slot(t, carry):
         for g in range(2):
-            u = t - 2 * (hops[g] - 1)
+            u = t - lag * (hops[g] - 1)
 
             @pl.when((hops[g] > 0) & (u >= 0) & (u < units))
             def _():
@@ -243,7 +245,7 @@
                 forward(g, units, True)
         return carry
 
-    lax.fori_loop(0, units + 1 + 2 * (last - 1), gather_slot, 0)
+    lax.fori_loop(0, units + 1 + lag * (last - 1), gather_slot, 0)
 
     def each_unit(action):
         def step(u, carry):
@@ -268,15 +270,27 @@
             agz_copy(g, units, True).wait_send()
 
 
-def update_kernel(width, place_ref, pat_ref, first_ref, second_ref, inverse_ref, model_ref, out_ref):
-    pats = pat_ref[...].T
-    columns = out_ref.shape[1]
-    for c in range(columns // width):
-        cols = slice(c * width, (c + 1) * width)
-        weights = jnp.concatenate([first_ref[0, :, cols], second_ref[0, :, cols]], axis=0)
-        numer = jnp.dot(pats, weights, preferred_element_type=F32)
-        numer += prior_weight * model_ref[:, cols].astype(F32)
-        out_ref[:, cols] = (numer * inverse_ref[:, cols]).astype(BF16)
+def update_kernel(width, tall, place_ref, pat_ref, first_ref, second_ref, inverse_ref, model_ref, out_ref):
+    pixels, columns = out_ref.shape
+    count = columns // width
+    deep = pat_ref.shape[0] // count
+
+    def turned(p, c):
+        return pat_ref[c * deep:(c + 1) * deep, p * tall:(p + 1) * tall].T
+
+    pieces = [turned(0, c) for c in range(count)]
+    for p in range(pixels // tall):
+        pats = jnp.concatenate(pieces, axis=1)
+        pieces = []
+        here = slice(p * tall, (p + 1) * tall)
+        for c in range(count):
+            cols = slice(c * width, (c + 1) * width)
+            weights = jnp.concatenate([first_ref[0, :, cols], second_ref[0, :, cols]], axis=0)
+            numer = jnp.dot(pats, weights, preferred_element_type=F32)
+            if (p + 1) * tall < pixels:
+                pieces.append(turned(p + 1, c))
+            numer += prior_weight * model_ref[here, cols].astype(F32)
+            out_ref[here, cols] = (numer * inverse_ref[:, cols]).astype(BF16)
 
 
 def local(n_pix, n_ori, patterns, model, scale_table, scale_index, weight_table, weight_class):
@@ -334,11 +348,11 @@
             bytes_accessed=2 * pixels * (rows + columns), transcendentals=rows * columns),
     )(patterns, model, phi, logw)
 
-    block = block_of(half_pix, 512)
+    block = block_of(half_pix, 1024)
     blocks = half_pix // block
     own_half = lax.axis_index("pat").astype(jnp.int32).reshape(1)
     return pl.pallas_call(
-        functools.partial(update_kernel, block_of(columns, 256)),
+        functools.partial(update_kernel, block_of(columns, 256), block_of(block, 512)),
         out_shape=jax.ShapeDtypeStruct((half_pix, columns), BF16),
         grid_spec=pltpu.PrefetchScalarGridSpec(
             num_scalar_prefetch=1,

time: 137 us -> 126 us (0.920)
  Pallas kernels: 121 us -> 110 us
    pallas_call x1, Pallas kernels: 91.5 us -> 84.1 us  [local(): pl.pallas_call(functools.partial(score_kernel, n_pix, n_ori, beta, chunks...]
    pallas_call x1, Pallas kernels: 29.1 us -> 25.5 us  [local(): pl.pallas_call(functools.partial(update_kernel, block_of(columns, 256), b...]
where the time goes in v5:
time: 126 us; the launch traced here: 125 us
  Pallas kernels  110 us (87%)
  between operations  13.4 us (11%)
    pallas_call x1, Pallas kernels, local(): pl.pallas_call(functools.partial(score_kernel, n_pix, n_ori, beta, chunks...  84.1 us
    pallas_call x1, Pallas kernels, local(): pl.pallas_call(functools.partial(update_kernel, block_of(columns, 256), b...  25.5 us
  transfers between devices with their start and end apart: 1, of which 0 were waited for; matrix products, arithmetic and copies ran while one was open for 1% of the time, Pallas kernels for 67%

profile of v5, /device:TPU:0, one launch (start us, length us, event | category | flops | bytes accessed | tf_op | source)
XLA Modules:
  0.0 125.4 jit_solution(2819900910697411915)
XLA Ops:
  6.5 0.0 copy-start.1
  6.5 0.0 copy-start.2
  6.5 0.0 copy-start
  6.5 0.0 copy-start.3
  6.5 0.0 all-gather.2.cloned.1.call-start
  6.6 0.7 all-gather.2.cloned.1.call-update
  7.3 0.0 copy-done.1
  7.3 0.0 copy-done.2
  7.3 0.1 select_reduce_fusion.1
  7.4 0.0 copy-done
  7.4 0.0 copy-done.3
  7.4 0.7 select_reduce_fusion
  8.1 0.8 broadcast_in_dim.41.phi_ref
  8.9 84.1 %shard_map.64 = (bf16[2,512,1024]{2,1,0:T(8,128)(2,1)}, f32[1,1024]{1,0:T(1,128)}) custom-call(bf16[512,16384]{1,0:T(8,128)(2,1)} %pat_hbm.1, bf16[16384,1024]{1,0:T(8,128)(2,1)} %model_ref.1, f32[512,128]{1,0:T(8,128)} %broadcast_in_dim.41.phi_ref, f32[1,1024]{1,0:T(1,128)} %bitcast.2), custom_call_target="tpu_custom_call" | custom-call | flops 17179869184 | bytes 50331648 | tf_op jit(solution)/shard_map/pallas_call | solution.py:315
  93.0 0.0 all-gather.2.cloned.1.call-done.pat_ref
  93.0 25.5 %shard_map.65 = bf16[8192,1024]{1,0:T(8,128)(2,1)} custom-call(s32[1]{0:T(128)} %bitcast.place_ref, bf16[1024,16384]{1,0:T(8,128)(2,1)} %all-gather.2.cloned.1.call-done.pat_ref, bf16[2,512,1024]{2,1,0:T(8,128)(2,1)} %get-tuple-element.7.first_ref.second_ref, bf16[2,512,1024]{2,1,0:T(8,128)(2,1)} %get-tuple-element.7.first_ref.second_ref, ...), custom_call_target="tpu_custom_call" | custom-call | flops 17179869184 | bytes 50331648 | tf_op jit(solution)/shard_map/pallas_call | solution.py:354
Async XLA Ops:
  6.5 0.7 copy-start.1
  6.5 0.8 copy-start.2
  6.5 0.8 copy-start
  6.5 0.8 copy-start.3
  6.5 86.5 %all-gather.2.cloned.1.call-start = ((), (), s32[]{:S(2)}) async-start(), calls=%async_computation | async-start | bytes 50331648 | tf_op jit(solution)/shard_map/all_gather | solution.py:314
Sparse Core Ops, SparseCore 0:
  8.9 53.9 all-gather.1
